TPU v7x, 32 devices: a whole 2x2x4 slice. The times are simulated.
32 devices in a mesh: group: 2 (over y), ctr: 4 (over x, core), dp: 4 (over z).
Axes of the slice: x: 2, y: 2, z: 4, core: 2. Of those that a mesh axis runs over, the one named last changes fastest.
Arguments:
- points: bfloat16 [32768, 256], P(('group', 'ctr', 'dp')), parts along dimension 0, may hold values from -6 to 6
- labels: bfloat16 [32768], P(('group', 'ctr', 'dp')), parts along dimension 0, may hold values from 0 to 2
- centre_index: int32 [1024], P(('group', 'ctr', 'dp')), parts along dimension 0, may hold values from 0 to 16383, as said below
- kernel_factor: float32 [1024, 512], P(('group', 'ctr')), parts along dimension 0, as said below
- ridge_factor: float32 [1024, 512], P(('group', 'ctr')), parts along dimension 0, as said below
Outputs:
- fitted: float32 [32768], P(('group', 'ctr', 'dp')), parts along dimension 0
There are 2 independent parts, one for each index of `group`. A program takes and returns all parts, laid end to end along the dimension named above; each array names one. Nothing has to cross between parts.
Inputs may be any that keep to these rules, and one draw needn't show every extreme that they name: `centre_index`: entry k lies in rows k * 32 to k * 32 + 31 of points. `kernel_factor`: upper triangular with a positive diagonal. `ridge_factor`: upper triangular with a positive diagonal.
All inputs are finite; a program needn't handle non-finite values.
Results may differ from a plain program's by a relative error of at most 0.004.
Values may be sent and summed in bfloat16 or wider, within the bound.
A program may use at most 64 MiB of HBM per device.

v0:
```python
import jax
import jax.numpy as jnp
from jax import lax
from jax.sharding import PartitionSpec as P

ITERS = 2


ridge_weight = 0.001


def kernel_block(point_rows, centres):
    feature_count = point_rows.shape[1]
    point_wide = point_rows.astype(jnp.float32)
    centre_wide = centres.astype(jnp.float32)
    point_sq = jnp.sum(point_wide * point_wide, axis=1)
    centre_sq = jnp.sum(centre_wide * centre_wide, axis=1)
    products = jnp.dot(point_rows, centres.T, preferred_element_type=jnp.float32)
    exponent = (2.0 * products - point_sq[:, None] - centre_sq[None, :]) * (2.0 / feature_count)
    return jnp.exp(exponent).astype(jnp.bfloat16)


def block_solve(factor_rows, vector, transposed):
    if transposed:
        partial_value = jnp.dot(vector, factor_rows, precision=lax.Precision.HIGHEST)
        return lax.psum_scatter(partial_value, "ctr", scatter_dimension=0, tiled=True)
    whole_vector = lax.all_gather(vector, "ctr", axis=0, tiled=True)
    return jnp.dot(factor_rows, whole_vector, precision=lax.Precision.HIGHEST)


def body(points, labels, centre_index, kernel_factor, ridge_factor):
    point_count = points.shape[0]
    first_row = (lax.axis_index("ctr") * lax.axis_size("dp") + lax.axis_index("dp")) * point_count
    chosen = jnp.take(points, centre_index - first_row, axis=0)
    centre_block = lax.all_gather(chosen, "dp", axis=0, tiled=True)
    all_points = point_count * lax.axis_size("ctr") * lax.axis_size("dp")

    def owner_sum(partial_value):
        owned = lax.psum_scatter(partial_value, "ctr", scatter_dimension=0, tiled=True)
        return lax.psum(owned, "dp")

    def kernel_values(shard_values):
        return jnp.dot(
            kernel_block(points, lax.all_gather(centre_block, "ctr", axis=0, tiled=True)),
            lax.all_gather(shard_values, "ctr", axis=0, tiled=True),
            preferred_element_type=jnp.float32,
        )

    def precondition(vector):
        scaled = block_solve(ridge_factor, vector, False)
        return (scaled, block_solve(kernel_factor, scaled, False))

    projected = owner_sum(
        jnp.dot(
            labels,
            kernel_block(points, lax.all_gather(centre_block, "ctr", axis=0, tiled=True)),
            preferred_element_type=jnp.float32,
        )
    )
    right_side = block_solve(
        ridge_factor, block_solve(kernel_factor, projected, True) / all_points, True
    )
    solution = jnp.zeros_like(right_side)
    residual = right_side

    def squares(vector):
        return lax.psum(jnp.sum(vector * vector), "ctr")

    direction = right_side
    norm_now = squares(residual)
    for iteration in range(ITERS):
        operator_scaled, lifted = precondition(direction)
        mapped = kernel_values(lifted.astype(jnp.bfloat16)).astype(jnp.bfloat16)
        summed = owner_sum(
            jnp.dot(
                mapped,
                kernel_block(points, lax.all_gather(centre_block, "ctr", axis=0, tiled=True)),
                preferred_element_type=jnp.float32,
            )
        )
        inner_side = (
            block_solve(kernel_factor, summed, True) / all_points + ridge_weight * operator_scaled
        )
        mapped = block_solve(ridge_factor, inner_side, True)
        step_size = norm_now / lax.psum(jnp.sum(direction * mapped), "ctr")
        solution = solution + step_size * direction
        residual = residual - step_size * mapped
        norm_next = squares(residual)
        direction = residual + norm_next / norm_now * direction
        norm_now = norm_next
    unused, coefficients = precondition(solution)
    return kernel_values(coefficients.astype(jnp.bfloat16))


def solution(mesh):
    in_specs = (
        P(("group", "ctr", "dp"), None),
        P(("group", "ctr", "dp")),
        P(("group", "ctr", "dp")),
        P(("group", "ctr"), None),
        P(("group", "ctr"), None),
    )
    out_specs = P(("group", "ctr", "dp"))
    return jax.shard_map(body, mesh=mesh, in_specs=in_specs, out_specs=out_specs, check_vma=False)
```

profile of v0, /device:TPU:0, one launch (start us, length us, event | category | flops | bytes accessed | tf_op | source)
XLA Modules:
  0.0 189.4 jit_solution(1936526678857602598)
XLA Ops:
  0.0 0.7 compare_and_fusion
  0.7 1.7 gather_fusion
  2.5 14.9 %all_gather.38 = bf16[128,256]{1,0:T(8,128)(2,1)S(1)} all-gather(bf16[32,256]{1,0:T(8,128)(2,1)S(1)} %broadcast_select_fusion), channel_id=1, replica_groups=mesh['group'=2,'ctr'=4,'dp'=4] {'dp'}, dimensions={0}, use_global_device_ids=true | all-gather | bytes 81920 | tf_op jit(solution)/shard_map/all_gather | solution.py:35
  17.4 5.8 %all_gather.39 = bf16[512,256]{1,0:T(8,128)(2,1)S(1)} all-gather(bf16[128,256]{1,0:T(8,128)(2,1)S(1)} %all_gather.38), channel_id=1, replica_groups=mesh['group'=2,'ctr'=4,'dp'=4] {'ctr'}, dimensions={0}, use_global_device_ids=true | all-gather | bytes 327680 | tf_op jit(solution)/shard_map/all_gather | solution.py:44
  23.6 0.6 fusion
  24.3 0.4 fusion.49
  24.7 7.1 %all-reduce = f32[512]{0:T(512)S(1)} all-reduce(f32[512]{0:T(512)S(1)} %bitcast.150), channel_id=2, replica_groups=mesh['group'=2,'ctr'=4,'dp'=4] {'ctr'}, use_global_device_ids=true, to_apply=%region_2.3.clone | all-reduce | flops 512 | bytes 4096
  31.8 0.6 dynamic-slice
  33.1 11.8 %psum.49 = f32[128]{0:T(128)S(1)} all-reduce(f32[128]{0:T(128)S(1)} %dynamic-slice.1), channel_id=1, replica_groups=mesh['group'=2,'ctr'=4,'dp'=4] {'dp'}, use_global_device_ids=true, to_apply=%region_3.4 | all-reduce | flops 128 | bytes 1024 | tf_op jit(solution)/shard_map/psum | solution.py:40
  45.1 5.9 %all-reduce.1 = f32[512]{0:T(512)S(1)} all-reduce(f32[512]{0:T(512)S(1)} %bitcast.151), channel_id=3, replica_groups=mesh['group'=2,'ctr'=4,'dp'=4] {'ctr'}, use_global_device_ids=true, to_apply=%region_4.5.clone | all-reduce | flops 512 | bytes 4096
  51.0 0.3 fusion.25
  51.3 5.7 %all-reduce.2 = f32[512]{0:T(512)S(1)} all-reduce(f32[512]{0:T(512)S(1)} %bitcast.152), channel_id=4, replica_groups=mesh['group'=2,'ctr'=4,'dp'=4] {'ctr'}, use_global_device_ids=true, to_apply=%region_5.6.clone | all-reduce | flops 512 | bytes 4096
  57.1 5.0 %all-gather = f32[4,1,128]{2,1,0:T(1,128)S(1)} all-gather(f32[1,1,128]{2,1,0:T(1,128)S(1)} %dynamic-slice_bitcast_fusion), channel_id=1, replica_groups=mesh['group'=2,'ctr'=4,'dp'=4] {'ctr'}, dimensions={0}, use_global_device_ids=true | all-gather | bytes 2560 | tf_op jit(solution)/shard_map/all_gather | solution.py:27
  62.1 0.3 fusion.19
  62.4 5.1 %all-gather.1 = f32[4,1,128]{2,1,0:T(1,128)S(1)} all-gather(f32[1,1,128]{2,1,0:T(1,128)S(1)} %bitcast.158), channel_id=1, replica_groups=mesh['group'=2,'ctr'=4,'dp'=4] {'ctr'}, dimensions={0}, use_global_device_ids=true | all-gather | bytes 2560 | tf_op jit(solution)/shard_map/all_gather | solution.py:27
  67.5 0.3 fusion.6
  67.7 5.1 %all-gather.2 = bf16[4,1,128]{2,1,0:T(2,128)(2,1)S(1)} all-gather(bf16[1,1,128]{2,1,0:T(2,128)(2,1)S(1)} %fusion.6), channel_id=1, replica_groups=mesh['group'=2,'ctr'=4,'dp'=4] {'ctr'}, dimensions={0}, use_global_device_ids=true | all-gather | bytes 1280 | tf_op jit(solution)/shard_map/all_gather | solution.py:45
  72.8 0.2 fusion.16
  73.1 0.4 fusion.50
  73.4 6.7 %all-reduce.3 = f32[512]{0:T(512)S(1)} all-reduce(f32[512]{0:T(512)S(1)} %bitcast.153), channel_id=5, replica_groups=mesh['group'=2,'ctr'=4,'dp'=4] {'ctr'}, use_global_device_ids=true, to_apply=%region_8.9.clone | all-reduce | flops 512 | bytes 4096
  80.2 8.3 %psum.51 = f32[128]{0:T(128)S(1)} all-reduce(f32[128]{0:T(128)S(1)} %dynamic-slice.7), channel_id=1, replica_groups=mesh['group'=2,'ctr'=4,'dp'=4] {'dp'}, use_global_device_ids=true, to_apply=%region_9.10 | all-reduce | flops 128 | bytes 1024 | tf_op jit(solution)/shard_map/psum | solution.py:40
  88.8 5.6 %all-reduce.4 = f32[512]{0:T(512)S(1)} all-reduce(f32[512]{0:T(512)S(1)} %bitcast.154), channel_id=6, replica_groups=mesh['group'=2,'ctr'=4,'dp'=4] {'ctr'}, use_global_device_ids=true, to_apply=%region_10.11.clone | all-reduce | flops 512 | bytes 4096
  94.4 0.3 fusion.32
  94.7 6.2 %all-reduce.5 = f32[512]{0:T(512)S(1)} all-reduce(f32[512]{0:T(512)S(1)} %bitcast.148), channel_id=7, replica_groups=mesh['group'=2,'ctr'=4,'dp'=4] {'ctr'}, use_global_device_ids=true, to_apply=%region_11.12.clone | all-reduce | flops 512 | bytes 4096
  100.9 0.8 multiply_reduce_fusion.3
  101.7 6.3 %all-reduce.9 = (f32[]{:T(128)}, f32[]{:T(128)}) all-reduce(f32[]{:T(128)} %get-tuple-element.6, f32[]{:T(128)} %get-tuple-element.5), channel_id=1, replica_groups=mesh['group'=2,'ctr'=4,'dp'=4] {'ctr'}, use_global_device_ids=true, to_apply=%region_7.8 | all-reduce | flops 2 | bytes 16 | tf_op jit(solution)/shard_map/psum | solution.py:67
  109.2 0.7 multiply_reduce_fusion.2
  109.9 7.1 %psum.53 = f32[]{:T(128)} all-reduce(f32[]{:T(128)} %multiply_reduce_fusion.2), channel_id=1, replica_groups=mesh['group'=2,'ctr'=4,'dp'=4] {'ctr'}, use_global_device_ids=true, to_apply=%region_15.16 | all-reduce | flops 1 | bytes 8 | tf_op jit(solution)/shard_map/psum | solution.py:67
  118.3 5.0 %all-gather.3 = f32[4,1,128]{2,1,0:T(1,128)S(1)} all-gather(f32[1,1,128]{2,1,0:T(1,128)S(1)} %bitcast.157), channel_id=1, replica_groups=mesh['group'=2,'ctr'=4,'dp'=4] {'ctr'}, dimensions={0}, use_global_device_ids=true | all-gather | bytes 2560 | tf_op jit(solution)/shard_map/all_gather | solution.py:27
  123.4 0.3 fusion.14
  123.6 5.1 %all-gather.4 = f32[4,1,128]{2,1,0:T(1,128)S(1)} all-gather(f32[1,1,128]{2,1,0:T(1,128)S(1)} %bitcast.159), channel_id=1, replica_groups=mesh['group'=2,'ctr'=4,'dp'=4] {'ctr'}, dimensions={0}, use_global_device_ids=true | all-gather | bytes 2560 | tf_op jit(solution)/shard_map/all_gather | solution.py:27
  128.7 0.3 fusion.4
  129.0 5.1 %all-gather.5 = bf16[4,1,128]{2,1,0:T(2,128)(2,1)S(1)} all-gather(bf16[1,1,128]{2,1,0:T(2,128)(2,1)S(1)} %fusion.4), channel_id=1, replica_groups=mesh['group'=2,'ctr'=4,'dp'=4] {'ctr'}, dimensions={0}, use_global_device_ids=true | all-gather | bytes 1280 | tf_op jit(solution)/shard_map/all_gather | solution.py:45
  134.1 0.2 fusion.11
  134.3 0.4 fusion.51
  134.7 6.4 %all-reduce.6 = f32[512]{0:T(512)S(1)} all-reduce(f32[512]{0:T(512)S(1)} %bitcast.155), channel_id=8, replica_groups=mesh['group'=2,'ctr'=4,'dp'=4] {'ctr'}, use_global_device_ids=true, to_apply=%region_16.17.clone | all-reduce | flops 512 | bytes 4096
  141.2 10.3 %psum.54 = f32[128]{0:T(128)S(1)} all-reduce(f32[128]{0:T(128)S(1)} %dynamic-slice.13), channel_id=1, replica_groups=mesh['group'=2,'ctr'=4,'dp'=4] {'dp'}, use_global_device_ids=true, to_apply=%region_17.18 | all-reduce | flops 128 | bytes 1024 | tf_op jit(solution)/shard_map/psum | solution.py:40
  151.8 5.6 %all-reduce.7 = f32[512]{0:T(512)S(1)} all-reduce(f32[512]{0:T(512)S(1)} %bitcast.156), channel_id=9, replica_groups=mesh['group'=2,'ctr'=4,'dp'=4] {'ctr'}, use_global_device_ids=true, to_apply=%region_18.19.clone | all-reduce | flops 512 | bytes 4096
  157.4 0.3 fusion.27
  157.7 6.5 %all-reduce.8 = f32[512]{0:T(512)S(1)} all-reduce(f32[512]{0:T(512)S(1)} %bitcast.149), channel_id=10, replica_groups=mesh['group'=2,'ctr'=4,'dp'=4] {'ctr'}, use_global_device_ids=true, to_apply=%region_19.20.clone | all-reduce | flops 512 | bytes 4096
  164.2 0.8 fusion.21
  165.0 6.3 %psum.55 = f32[]{:T(128)} all-reduce(f32[]{:T(128)} %fusion.21), channel_id=1, replica_groups=mesh['group'=2,'ctr'=4,'dp'=4] {'ctr'}, use_global_device_ids=true, to_apply=%region_21.22 | all-reduce | flops 1 | bytes 8 | tf_op jit(solution)/shard_map/psum | solution.py:85
  172.8 5.0 %all-gather.6 = f32[4,1,128]{2,1,0:T(1,128)S(1)} all-gather(f32[1,1,128]{2,1,0:T(1,128)S(1)} %add_bitcast_fusion), channel_id=1, replica_groups=mesh['group'=2,'ctr'=4,'dp'=4] {'ctr'}, dimensions={0}, use_global_device_ids=true | all-gather | bytes 2560 | tf_op jit(solution)/shard_map/all_gather | solution.py:27
  177.8 0.3 convolution_bitcast_fusion.1
  178.1 5.1 %all-gather.7 = f32[4,1,128]{2,1,0:T(1,128)S(1)} all-gather(f32[1,1,128]{2,1,0:T(1,128)S(1)} %convolution_bitcast_fusion.1), channel_id=1, replica_groups=mesh['group'=2,'ctr'=4,'dp'=4] {'ctr'}, dimensions={0}, use_global_device_ids=true | all-gather | bytes 2560 | tf_op jit(solution)/shard_map/all_gather | solution.py:27
  183.2 0.3 fusion.2
  183.4 5.1 %all-gather.8 = bf16[4,1,128]{2,1,0:T(2,128)(2,1)S(1)} all-gather(bf16[1,1,128]{2,1,0:T(2,128)(2,1)S(1)} %fusion.2), channel_id=1, replica_groups=mesh['group'=2,'ctr'=4,'dp'=4] {'ctr'}, dimensions={0}, use_global_device_ids=true | all-gather | bytes 1280 | tf_op jit(solution)/shard_map/all_gather | solution.py:45
  188.5 0.8 fusion.7
  (28 shorter events, 1.7 us)
Async XLA Ops:
  0.0 51.0 %copy-start = (f32[128,512]{1,0:T(8,128)S(1)}, f32[128,512]{1,0:T(8,128)}, u32[]{:S(2)}) copy-start(f32[128,512]{1,0:T(8,128)} %param.9) | copy-start | bytes 786436
  0.0 23.4 %copy-start.2 = (bf16[1024,256]{1,0:T(8,128)(2,1)S(1)}, bf16[1024,256]{1,0:T(8,128)(2,1)}, u32[]{:S(2)}) copy-start(bf16[1024,256]{1,0:T(8,128)(2,1)} %param.5) | copy-start | bytes 1572868
  23.6 0.7 copy-start.3
  24.3 7.5 %copy-start.4 = (u32[32]{0:T(128)S(1)}, u32[32]{0:T(128)}, u32[]{:S(2)}) copy-start(u32[32]{0:T(128)} %constant.41) | copy-start | bytes 388
  24.3 20.6 %copy-start.1 = (f32[128,512]{1,0:T(8,128)S(1)}, f32[128,512]{1,0:T(8,128)}, u32[]{:S(2)}) copy-start(f32[128,512]{1,0:T(8,128)} %param.8) | copy-start | bytes 786436
where the time goes:
time: 190 us; the launch traced here: 189 us
  blocking collectives  172 us (91%)
  matrix products  6.21 us (3%)
  between operations  4.63 us (2%)
  other arithmetic  3.54 us (2%)
  local copies, waits for them, and re-layouts  2.66 us (1%)
    unnamed x9, blocking collectives  55.8 us
    psum x3, blocking collectives, owner_sum(): return lax.psum(owned, 'dp')  30.5 us
    all_gather x6, blocking collectives, block_solve(): whole_vector = lax.all_gather(vector, 'ctr', axis=0, tiled=True)  30.4 us
    all_gather x3, blocking collectives, kernel_values(): lax.all_gather(shard_values, 'ctr', axis=0, tiled=True)  15.3 us
    all_gather x1, blocking collectives, body(): centre_block = lax.all_gather(chosen, 'dp', axis=0, tiled=True)  14.9 us
    psum x2, blocking collectives, squares(): return lax.psum(jnp.sum(vector * vector), 'ctr')  13.4 us
    psum x1, blocking collectives, body(): step_size = norm_now / lax.psum(jnp.sum(direction * mapped), 'ctr')  6.35 us
    all_gather x1, blocking collectives, kernel_values(): lax.all_gather(centre_block, 'ctr', axis=0, tiled=True)  5.77 us

commit v1 on v0

v1 whole, which is shorter than its diff:
```python
import functools

import jax
import jax.numpy as jnp
from jax import lax
from jax.experimental import pallas as pl
from jax.experimental.pallas import tpu as pltpu
from jax.sharding import PartitionSpec as P

ITERS = 2
RIDGE = 0.001
MESH = pl.DeviceIdType.MESH
F32 = jnp.float32
BF16 = jnp.bfloat16
NT = (((1,), (1,)), ((), ()))


def kernel(nc, nd, pts, lab, idx, kf, rf, out,
           cbuf, kt, rbuf, tbuf, zbuf, xbuf,
           c1s, c1r, c2s, c2r, fs, fr, zs, zr, xs, xr):
    n_pts, feats = pts.shape
    per = idx.shape[1]
    half = feats // 2
    cb = per * nd
    m = cb * nc
    all_points = float(n_pts * nc * nd)
    c = lax.axis_index("ctr")
    d = lax.axis_index("dp")

    barrier = pltpu.get_barrier_semaphore()
    for k in range(1, nd):
        pl.semaphore_signal(barrier, inc=1, device_id={"dp": lax.rem(d + k, nd)}, device_id_type=MESH)
    for k in range(1, nc):
        pl.semaphore_signal(barrier, inc=1, device_id={"ctr": lax.rem(c + k, nc)}, device_id_type=MESH)

    first = (c * nd + d) * n_pts
    local = (idx[...] - first).astype(F32)
    square = lax.broadcasted_iota(jnp.int32, (per, per), 0) == lax.broadcasted_iota(jnp.int32, (per, per), 1)
    local = jnp.sum(jnp.where(square, local, 0.0), axis=1, keepdims=True).astype(jnp.int32)
    places = lax.broadcasted_iota(jnp.int32, (per, n_pts), 1)
    onehot = jnp.where(places == local, 1.0, 0.0).astype(BF16)
    chosen = jnp.dot(onehot, pts[...], preferred_element_type=F32)
    cbuf[c, d] = jnp.concatenate([chosen[:, :half], chosen[:, half:]], axis=0).astype(BF16)

    rbuf[c] = rf[...]
    tbuf[c] = kf[...].T

    pl.semaphore_wait(barrier, nc + nd - 2)

    def spread(ref_src, axis, me, n, send, recv):
        copies = []
        for k in range(1, n):
            copy = pltpu.make_async_remote_copy(
                src_ref=ref_src, dst_ref=ref_src, send_sem=send.at[k - 1], recv_sem=recv.at[k - 1],
                device_id={axis: lax.rem(me + k, n)}, device_id_type=MESH)
            copy.start()
            copies.append(copy)
        return copies

    sent = []
    first_copies = spread(cbuf.at[c, d], "dp", d, nd, c1s, c1r)
    sent += first_copies

    def factor_copies(cc):
        made = []
        for k in range(1, nc):
            peer = (cc + k) % nc
            for which, ref in ((0, tbuf.at[cc, pl.ds(cb * cc, m - cb * cc)]),
                               (1, rbuf.at[cc, :, pl.ds(cb * cc, m - cb * cc)])):
                made.append(pltpu.make_async_remote_copy(
                    src_ref=ref, dst_ref=ref, send_sem=fs.at[which, k - 1], recv_sem=fr.at[which, k - 1],
                    device_id={"ctr": peer}, device_id_type=MESH))
        return made

    def factor_sources(cc):
        made = []
        for k in range(1, nc):
            src = (cc - k) % nc
            for which, ref in ((0, tbuf.at[src, pl.ds(cb * src, m - cb * src)]),
                               (1, rbuf.at[src, :, pl.ds(cb * src, m - cb * src)])):
                made.append(pltpu.make_async_remote_copy(
                    src_ref=ref, dst_ref=ref, send_sem=fs.at[which, k - 1], recv_sem=fr.at[which, k - 1],
                    device_id={"ctr": src}, device_id_type=MESH))
        return made

    wide = pts[...].astype(F32)
    sq = wide * wide
    sq_hi = sq.astype(BF16)
    sq_lo = (sq - sq_hi.astype(F32)).astype(BF16)
    ones = jnp.ones((8, feats), BF16)
    point_sq = (lax.dot_general(ones, sq_hi, NT, preferred_element_type=F32)
                + lax.dot_general(ones, sq_lo, NT, preferred_element_type=F32))[:1]

    for copy in first_copies:
        copy.wait_recv()
    second_copies = spread(cbuf.at[c], "ctr", c, nc, c2s, c2r)
    sent += second_copies

    for cc in range(nc):
        @pl.when(c == cc)
        def _(cc=cc):
            for copy in factor_copies(cc):
                copy.start()

    def form(owner):
        block = cbuf[owner].astype(F32).reshape(nd, 2, per, half)
        left = block[:, 0].reshape(cb, half)
        right = block[:, 1].reshape(cb, half)
        centre_sq = jnp.sum(left * left + right * right, axis=1, keepdims=True)
        centres = jnp.concatenate([left, right], axis=1).astype(BF16)
        products = lax.dot_general(centres, pts[...], NT, preferred_element_type=F32)
        exponent = (2.0 * products - point_sq - centre_sq) * (2.0 / feats)
        kt[pl.ds(pl.multiple_of(owner * cb, cb), cb), :] = jnp.exp(exponent).astype(BF16)

    form(c)
    for k in range(1, nc):
        second_copies[k - 1].wait_recv()
        form(lax.rem(c - k + nc, nc))

    def total(r, part):
        zbuf[r, d] = part
        copies = spread(zbuf.at[r, d], "dp", d, nd, zs.at[r], zr.at[r])
        for copy in copies:
            copy.wait_recv()
        acc = zbuf[r, 0]
        for k in range(1, nd):
            acc = acc + zbuf[r, k]
        xbuf[r, c] = acc
        more = spread(xbuf.at[r, c], "ctr", c, nc, xs.at[r], xr.at[r])
        for copy in more:
            copy.wait_recv()
        acc = xbuf[r, 0]
        for k in range(1, nc):
            acc = acc + xbuf[r, k]
        sent.extend(copies + more)
        return acc

    def ridge_solve(row):
        return [jnp.sum(rbuf[b, :, cb * b:] * row[:, cb * b:], axis=1, keepdims=True) for b in range(nc)]

    def ridge_solve_transposed(column):
        parts = [0.0] * nc
        for b in range(nc):
            for j in range(b, nc):
                prod = rbuf[b, :, cb * j:cb * (j + 1)] * column[b]
                parts[j] = parts[j] + prod
        return jnp.concatenate([jnp.sum(p, axis=0, keepdims=True) for p in parts], axis=1)

    def kernel_solve(column):
        rows = []
        for b in range(nc):
            acc = 0.0
            for j in range(b, nc):
                acc = acc + tbuf[b, cb * j:cb * (j + 1), :] * column[j]
            rows.append(jnp.sum(acc, axis=0, keepdims=True))
        return jnp.concatenate(rows, axis=1)

    def kernel_solve_transposed(row):
        columns = []
        for j in range(nc):
            acc = 0.0
            for b in range(j + 1):
                acc = acc + tbuf[b, cb * j:cb * (j + 1), :] * row[:, cb * b:cb * (b + 1)]
            columns.append(jnp.sum(acc, axis=1, keepdims=True))
        return columns

    def to_centres(row):
        return lax.dot_general(row, kt[...], NT, preferred_element_type=F32)

    def to_points(row):
        return jnp.dot(row, kt[...], preferred_element_type=F32)

    summed = total(0, to_centres(lab[...]))
    for cc in range(nc):
        @pl.when(c == cc)
        def _(cc=cc):
            for copy in factor_sources(cc):
                copy.wait_recv()
    right_side = ridge_solve_transposed(kernel_solve_transposed(summed / all_points))
    beta = jnp.zeros_like(right_side)
    residual = right_side
    direction = right_side
    norm_now = jnp.sum(residual * residual, axis=1, keepdims=True)
    for iteration in range(ITERS):
        scaled = ridge_solve(direction)
        lifted = kernel_solve(scaled).astype(BF16)
        image = to_points(lifted).astype(BF16)
        summed = total(1 + iteration, to_centres(image))
        inner = kernel_solve_transposed(summed / all_points)
        mapped = ridge_solve_transposed([a + RIDGE * s for a, s in zip(inner, scaled)])
        step = norm_now / jnp.sum(direction * mapped, axis=1, keepdims=True)
        beta = beta + step * direction
        residual = residual - step * mapped
        norm_next = jnp.sum(residual * residual, axis=1, keepdims=True)
        direction = residual + (norm_next / norm_now) * direction
        norm_now = norm_next
    coefficients = kernel_solve(ridge_solve(beta)).astype(BF16)
    out[...] = to_points(coefficients)

    for copy in sent:
        copy.wait_send()
    for cc in range(nc):
        @pl.when(c == cc)
        def _(cc=cc):
            for copy in factor_copies(cc):
                copy.wait_send()


def solution(mesh):
    nc, nd = mesh.shape["ctr"], mesh.shape["dp"]

    def body(points, labels, centre_index, kernel_factor, ridge_factor):
        n_pts, feats = points.shape
        per = centre_index.shape[0]
        cb = kernel_factor.shape[0]
        m = cb * nc
        dma = pltpu.SemaphoreType.DMA
        rounds = ITERS + 1
        fitted = pl.pallas_call(
            functools.partial(kernel, nc, nd),
            out_shape=jax.ShapeDtypeStruct((1, n_pts), F32),
            in_specs=[pl.BlockSpec(memory_space=pltpu.VMEM)] * 5,
            out_specs=pl.BlockSpec(memory_space=pltpu.VMEM),
            scratch_shapes=[
                pltpu.VMEM((nc, nd, 2 * per, feats // 2), BF16),
                pltpu.VMEM((m, n_pts), BF16),
                pltpu.VMEM((nc, cb, m), F32),
                pltpu.VMEM((nc, m, cb), F32),
                pltpu.VMEM((rounds, nd, 1, m), F32),
                pltpu.VMEM((rounds, nc, 1, m), F32),
                dma((nd - 1,)), dma((nd - 1,)),
                dma((nc - 1,)), dma((nc - 1,)),
                dma((2, nc - 1)), dma((2, nc - 1)),
                dma((rounds, nd - 1)), dma((rounds, nd - 1)),
                dma((rounds, nc - 1)), dma((rounds, nc - 1)),
            ],
            compiler_params=pltpu.CompilerParams(
                collective_id=0, has_side_effects=True, vmem_limit_bytes=56 * 2**20),
        )(points, labels.reshape(1, -1), centre_index.reshape(1, -1), kernel_factor, ridge_factor)
        return fitted.reshape(-1)

    whole = ("group", "ctr", "dp")
    in_specs = (P(whole, None), P(whole), P(whole), P(("group", "ctr"), None), P(("group", "ctr"), None))
    return jax.shard_map(body, mesh=mesh, in_specs=in_specs, out_specs=P(whole), check_vma=False)
```

time: 190 us -> 50 us (0.26)
  blocking collectives: 172 us -> 0 us
  Pallas kernels: 0 us -> 47 us
  matrix products: 6.21 us -> 0 us
  between operations: 4.63 us -> 0.01 us
  other arithmetic: 3.54 us -> 0 us
    all_gather x11 -> x0, blocking collectives: 66.3 us -> none  [the longest x6 30.4 us: block_solve(): whole_vector = lax.all_gather(vector, 'ctr', axis=0, tiled=True)]
    unnamed x9 -> x0, blocking collectives: 55.8 us -> none
    psum x6 -> x0, blocking collectives: 50.2 us -> none  [the longest x3 30.5 us: owner_sum(): return lax.psum(owned, 'dp')]
    pallas_call x0 -> x1, Pallas kernels: none -> 47 us  [body(): pl.pallas_call(functools.partial(kernel, nc, nd), out_shape=jax.ShapeDtyp...]
    dot_general x19 -> x0, matrix products: 6.21 us -> none  [the longest x6 1.57 us: block_solve(): return jnp.dot(factor_rows, whole_vector, precision=lax.Precision.HIGHEST)]
    reduce_sum x5 -> x0, other arithmetic: 2.55 us -> none  [the longest x2 1.51 us: body(): step_size = norm_now / lax.psum(jnp.sum(direction * mapped), 'ctr')]
where the time goes in v1:
time: 50 us; the launch traced here: 49.6 us
  Pallas kernels  47 us (94%)
  local copies, waits for them, and re-layouts  2.55 us (5%)
    pallas_call x1, Pallas kernels, body(): pl.pallas_call(functools.partial(kernel, nc, nd), out_shape=jax.ShapeDtyp...  47 us
    reshape x1, local copies, waits for them, and re-layouts, body(): labels.reshape(1, -1)  1.28 us
    unnamed x1, local copies, waits for them, and re-layouts  1.28 us

profile of v1, /device:TPU:0, one launch (start us, length us, event | category | flops | bytes accessed | tf_op | source)
XLA Modules:
  0.0 49.6 jit_solution(16347720528477176223)
XLA Ops:
  0.0 1.3 %reshape.9.lab = bf16[1,1024]{1,0:T(2,128)(2,1)} reshape(bf16[1024]{0:T(1024)(128)(2,1)} %param.6) | data formatting | bytes 4096 | tf_op jit(solution)/shard_map/reshape | solution.py:239
  1.3 47.0 %shard_map.55 = f32[1,1024]{1,0:T(1,128)} custom-call(bf16[1024,256]{1,0:T(8,128)(2,1)} %pts.1, bf16[1,1024]{1,0:T(2,128)(2,1)} %reshape.9.lab, s32[1,32]{1,0:T(1,128)} %bitcast.3, f32[128,512]{1,0:T(8,128)} %kf.1, f32[128,512]{1,0:T(8,128)} %rf.1), custom_call_target="tpu_custom_call" | custom-call | tf_op jit(solution)/shard_map/pallas_call | solution.py:219
  48.3 1.3 %copy.7 = f32[1024]{0:T(1024)} copy(f32[1024]{0:T(1024)} %bitcast.2) | data formatting | bytes 8192

commit v2 on v1

--- a/solution.py
+++ b/solution.py
@@ -15,9 +15,9 @@
 NT = (((1,), (1,)), ((), ()))
 
 
-def kernel(nc, nd, pts, lab, idx, kf, rf, out,
-           cbuf, kt, rbuf, tbuf, zbuf, xbuf,
-           c1s, c1r, c2s, c2r, fs, fr, zs, zr, xs, xr):
+def kernel(nc, nd, flat, pts_in, lab_in, idx_in, kf_in, rf_in, out,
+           pts, lab, idx, kf, cbuf, kt, rbuf, tbuf, zbuf, xbuf,
+           ins, c1s, c1r, c2s, c2r, fs, fr, zs, zr, xs, xr):
     n_pts, feats = pts.shape
     per = idx.shape[1]
     half = feats // 2
@@ -27,13 +27,19 @@
     c = lax.axis_index("ctr")
     d = lax.axis_index("dp")
 
+    others = [(kc, kd) for kc in range(nc) for kd in range(nd) if (kc or kd) and (flat or not (kc and kd))]
     barrier = pltpu.get_barrier_semaphore()
-    for k in range(1, nd):
-        pl.semaphore_signal(barrier, inc=1, device_id={"dp": lax.rem(d + k, nd)}, device_id_type=MESH)
-    for k in range(1, nc):
-        pl.semaphore_signal(barrier, inc=1, device_id={"ctr": lax.rem(c + k, nc)}, device_id_type=MESH)
+    for kc, kd in others:
+        pl.semaphore_signal(barrier, inc=1, device_id_type=MESH,
+                            device_id={"ctr": lax.rem(c + kc, nc), "dp": lax.rem(d + kd, nd)})
+    loads = [pltpu.make_async_copy(a, b, ins.at[i]) for i, (a, b) in enumerate(
+        ((idx_in, idx), (pts_in, pts), (kf_in, kf), (rf_in, rbuf.at[c]), (lab_in, lab)))]
+    for load in loads:
+        load.start()
 
     first = (c * nd + d) * n_pts
+    loads[0].wait()
+    loads[1].wait()
     local = (idx[...] - first).astype(F32)
     square = lax.broadcasted_iota(jnp.int32, (per, per), 0) == lax.broadcasted_iota(jnp.int32, (per, per), 1)
     local = jnp.sum(jnp.where(square, local, 0.0), axis=1, keepdims=True).astype(jnp.int32)
@@ -42,10 +48,12 @@
     chosen = jnp.dot(onehot, pts[...], preferred_element_type=F32)
     cbuf[c, d] = jnp.concatenate([chosen[:, :half], chosen[:, half:]], axis=0).astype(BF16)
 
-    rbuf[c] = rf[...]
+    loads[2].wait()
     tbuf[c] = kf[...].T
-
-    pl.semaphore_wait(barrier, nc + nd - 2)
+    loads[3].wait()
+    loads[4].wait()
+
+    pl.semaphore_wait(barrier, len(others))
 
     def spread(ref_src, axis, me, n, send, recv):
         copies = []
@@ -61,27 +69,49 @@
     first_copies = spread(cbuf.at[c, d], "dp", d, nd, c1s, c1r)
     sent += first_copies
 
-    def factor_copies(cc):
-        made = []
-        for k in range(1, nc):
-            peer = (cc + k) % nc
-            for which, ref in ((0, tbuf.at[cc, pl.ds(cb * cc, m - cb * cc)]),
-                               (1, rbuf.at[cc, :, pl.ds(cb * cc, m - cb * cc)])):
-                made.append(pltpu.make_async_remote_copy(
-                    src_ref=ref, dst_ref=ref, send_sem=fs.at[which, k - 1], recv_sem=fr.at[which, k - 1],
-                    device_id={"ctr": peer}, device_id_type=MESH))
-        return made
-
-    def factor_sources(cc):
-        made = []
-        for k in range(1, nc):
-            src = (cc - k) % nc
-            for which, ref in ((0, tbuf.at[src, pl.ds(cb * src, m - cb * src)]),
-                               (1, rbuf.at[src, :, pl.ds(cb * src, m - cb * src)])):
-                made.append(pltpu.make_async_remote_copy(
-                    src_ref=ref, dst_ref=ref, send_sem=fs.at[which, k - 1], recv_sem=fr.at[which, k - 1],
-                    device_id={"ctr": src}, device_id_type=MESH))
-        return made
+    def factor_copy(which, block, to, send):
+        rest = pl.ds(cb * block, m - cb * block)
+        ref = rbuf.at[block, :, rest] if which else tbuf.at[block, rest]
+        return pltpu.make_async_remote_copy(
+            src_ref=ref, dst_ref=ref, send_sem=fs.at[which, send], recv_sem=fr.at[which, block],
+            device_id={"ctr": to}, device_id_type=MESH)
+
+    def same_core(cc):
+        return [(cc + k) % nc for k in range(2, nc, 2)]
+
+    def direct(cc, which):
+        return [factor_copy(which, cc, p, p) for p in same_core(cc) + [cc ^ 1]]
+
+    def handed(cc, which):
+        return [factor_copy(which, p, cc ^ 1, nc + p) for p in same_core(cc)]
+
+    def arriving(cc, which):
+        return [factor_copy(which, p, p, p) for p in same_core(cc ^ 1) + [cc ^ 1]]
+
+    def on_each(action):
+        for cc in range(nc):
+            pl.when(c == cc)(functools.partial(action, cc))
+
+    def factors_start(cc):
+        for which in range(2):
+            for copy in direct(cc, which):
+                copy.start()
+
+    def factors_hand_on(cc):
+        for which in range(2):
+            for p in same_core(cc):
+                factor_copy(which, p, p, p).wait_recv()
+            for copy in handed(cc, which):
+                copy.start()
+
+    def factors_arrive(which, cc):
+        for copy in arriving(cc, which):
+            copy.wait_recv()
+
+    def factors_end(cc):
+        for which in range(2):
+            for copy in direct(cc, which) + handed(cc, which):
+                copy.wait_send()
 
     wide = pts[...].astype(F32)
     sq = wide * wide
@@ -96,11 +126,7 @@
     second_copies = spread(cbuf.at[c], "ctr", c, nc, c2s, c2r)
     sent += second_copies
 
-    for cc in range(nc):
-        @pl.when(c == cc)
-        def _(cc=cc):
-            for copy in factor_copies(cc):
-                copy.start()
+    on_each(factors_start)
 
     def form(owner):
         block = cbuf[owner].astype(F32).reshape(nd, 2, per, half)
@@ -117,23 +143,35 @@
         second_copies[k - 1].wait_recv()
         form(lax.rem(c - k + nc, nc))
 
-    def total(r, part):
-        zbuf[r, d] = part
-        copies = spread(zbuf.at[r, d], "dp", d, nd, zs.at[r], zr.at[r])
+    def total(r, part, meanwhile=None):
+        if flat:
+            zbuf[r, c, d] = part
+            copies = []
+            for i, (kc, kd) in enumerate(others):
+                copy = pltpu.make_async_remote_copy(
+                    src_ref=zbuf.at[r, c, d], dst_ref=zbuf.at[r, c, d],
+                    send_sem=zs.at[r, i], recv_sem=zr.at[r, i], device_id_type=MESH,
+                    device_id={"ctr": lax.rem(c + kc, nc), "dp": lax.rem(d + kd, nd)})
+                copy.start()
+                copies.append(copy)
+            if meanwhile is not None:
+                meanwhile()
+            for copy in copies:
+                copy.wait_recv()
+            sent.extend(copies)
+            return jnp.sum(zbuf[r].reshape(nc * nd, m), axis=0, keepdims=True)
+        zbuf[r, 0, d] = part
+        copies = spread(zbuf.at[r, 0, d], "dp", d, nd, zs.at[r], zr.at[r])
         for copy in copies:
             copy.wait_recv()
-        acc = zbuf[r, 0]
-        for k in range(1, nd):
-            acc = acc + zbuf[r, k]
-        xbuf[r, c] = acc
+        xbuf[r, c] = jnp.sum(zbuf[r, 0].reshape(nd, m), axis=0, keepdims=True)
         more = spread(xbuf.at[r, c], "ctr", c, nc, xs.at[r], xr.at[r])
+        if meanwhile is not None:
+            meanwhile()
         for copy in more:
             copy.wait_recv()
-        acc = xbuf[r, 0]
-        for k in range(1, nc):
-            acc = acc + xbuf[r, k]
         sent.extend(copies + more)
-        return acc
+        return jnp.sum(xbuf[r].reshape(nc, m), axis=0, keepdims=True)
 
     def ridge_solve(row):
         return [jnp.sum(rbuf[b, :, cb * b:] * row[:, cb * b:], axis=1, keepdims=True) for b in range(nc)]
@@ -170,13 +208,12 @@
     def to_points(row):
         return jnp.dot(row, kt[...], preferred_element_type=F32)
 
-    summed = total(0, to_centres(lab[...]))
-    for cc in range(nc):
-        @pl.when(c == cc)
-        def _(cc=cc):
-            for copy in factor_sources(cc):
-                copy.wait_recv()
-    right_side = ridge_solve_transposed(kernel_solve_transposed(summed / all_points))
+    label_row = jnp.concatenate([lab[r:r + 1, :] for r in range(n_pts // 128)], axis=1)
+    summed = total(0, to_centres(label_row), lambda: on_each(factors_hand_on))
+    on_each(functools.partial(factors_arrive, 0))
+    lowered = kernel_solve_transposed(summed / all_points)
+    on_each(functools.partial(factors_arrive, 1))
+    right_side = ridge_solve_transposed(lowered)
     beta = jnp.zeros_like(right_side)
     residual = right_side
     direction = right_side
@@ -199,11 +236,7 @@
 
     for copy in sent:
         copy.wait_send()
-    for cc in range(nc):
-        @pl.when(c == cc)
-        def _(cc=cc):
-            for copy in factor_copies(cc):
-                copy.wait_send()
+    on_each(factors_end)
 
 
 def solution(mesh):
@@ -216,27 +249,35 @@
         m = cb * nc
         dma = pltpu.SemaphoreType.DMA
         rounds = ITERS + 1
+        flat = nc * nd <= 32
+        rows = nc if flat else 1
+        links = nc * nd - 1 if flat else nd - 1
         fitted = pl.pallas_call(
-            functools.partial(kernel, nc, nd),
+            functools.partial(kernel, nc, nd, flat),
             out_shape=jax.ShapeDtypeStruct((1, n_pts), F32),
-            in_specs=[pl.BlockSpec(memory_space=pltpu.VMEM)] * 5,
+            in_specs=[pl.BlockSpec(memory_space=pl.ANY)] * 5,
             out_specs=pl.BlockSpec(memory_space=pltpu.VMEM),
             scratch_shapes=[
+                pltpu.VMEM((n_pts, feats), BF16),
+                pltpu.VMEM((n_pts // 128, 128), BF16),
+                pltpu.VMEM((1, per), jnp.int32),
+                pltpu.VMEM((cb, m), F32),
                 pltpu.VMEM((nc, nd, 2 * per, feats // 2), BF16),
                 pltpu.VMEM((m, n_pts), BF16),
                 pltpu.VMEM((nc, cb, m), F32),
                 pltpu.VMEM((nc, m, cb), F32),
-                pltpu.VMEM((rounds, nd, 1, m), F32),
+                pltpu.VMEM((rounds, rows, nd, 1, m), F32),
                 pltpu.VMEM((rounds, nc, 1, m), F32),
+                dma((5,)),
                 dma((nd - 1,)), dma((nd - 1,)),
                 dma((nc - 1,)), dma((nc - 1,)),
-                dma((2, nc - 1)), dma((2, nc - 1)),
-                dma((rounds, nd - 1)), dma((rounds, nd - 1)),
+                dma((2, 2 * nc)), dma((2, nc)),
+                dma((rounds, links)), dma((rounds, links)),
                 dma((rounds, nc - 1)), dma((rounds, nc - 1)),
             ],
             compiler_params=pltpu.CompilerParams(
                 collective_id=0, has_side_effects=True, vmem_limit_bytes=56 * 2**20),
-        )(points, labels.reshape(1, -1), centre_index.reshape(1, -1), kernel_factor, ridge_factor)
+        )(points, labels.reshape(-1, 128), centre_index.reshape(1, -1), kernel_factor, ridge_factor)
         return fitted.reshape(-1)
 
     whole = ("group", "ctr", "dp")

time: 50 us -> 37.7 us (0.75)
  Pallas kernels: 47 us -> 36.2 us
  local copies, waits for them, and re-layouts: 2.55 us -> 1.28 us
    pallas_call x1, Pallas kernels: 47 us -> 36.2 us  [body(): pl.pallas_call(functools.partial(kernel, nc, nd, flat), out_shape=jax.Sha...]
    reshape x1 -> x0, local copies, waits for them, and re-layouts: 1.28 us -> none  [body(): labels.reshape(1, -1)]
where the time goes in v2:
time: 37.7 us; the launch traced here: 37.5 us
  Pallas kernels  36.2 us (96%)
  local copies, waits for them, and re-layouts  1.28 us (3%)
    pallas_call x1, Pallas kernels, body(): pl.pallas_call(functools.partial(kernel, nc, nd, flat), out_shape=jax.Sha...  36.2 us
    unnamed x1, local copies, waits for them, and re-layouts  1.28 us

profile of v2, /device:TPU:0, one launch (start us, length us, event | category | flops | bytes accessed | tf_op | source)
XLA Modules:
  0.0 37.5 jit_solution(17461333599720414948)
XLA Ops:
  0.0 36.2 %shard_map.55 = f32[1,1024]{1,0:T(1,128)} custom-call(bf16[1024,256]{1,0:T(8,128)(2,1)} %pts_in.1, bf16[8,128]{1,0:T(8,128)(2,1)} %bitcast.4, s32[1,32]{1,0:T(1,128)} %bitcast.5, f32[128,512]{1,0:T(8,128)} %kf_in.1, f32[128,512]{1,0:T(8,128)} %rf_in.1), custom_call_target="tpu_custom_call" | custom-call | tf_op jit(solution)/shard_map/pallas_call | solution.py:255
  36.3 1.3 %copy.7 = f32[1024]{0:T(1024)} copy(f32[1024]{0:T(1024)} %bitcast.3) | data formatting | bytes 8192

commit v3 on v2

--- a/solution.py
+++ b/solution.py
@@ -27,9 +27,10 @@
     c = lax.axis_index("ctr")
     d = lax.axis_index("dp")
 
-    others = [(kc, kd) for kc in range(nc) for kd in range(nd) if (kc or kd) and (flat or not (kc and kd))]
+    others = [(kc, kd) for kc in range(nc) for kd in range(nd) if kc or kd]
+    near = [(kc, kd) for kc, kd in others if not (kc and kd)]
     barrier = pltpu.get_barrier_semaphore()
-    for kc, kd in others:
+    for kc, kd in near:
         pl.semaphore_signal(barrier, inc=1, device_id_type=MESH,
                             device_id={"ctr": lax.rem(c + kc, nc), "dp": lax.rem(d + kd, nd)})
     loads = [pltpu.make_async_copy(a, b, ins.at[i]) for i, (a, b) in enumerate(
@@ -53,7 +54,7 @@
     loads[3].wait()
     loads[4].wait()
 
-    pl.semaphore_wait(barrier, len(others))
+    pl.semaphore_wait(barrier, len(near))
 
     def spread(ref_src, axis, me, n, send, recv):
         copies = []
@@ -92,17 +93,15 @@
         for cc in range(nc):
             pl.when(c == cc)(functools.partial(action, cc))
 
-    def factors_start(cc):
-        for which in range(2):
-            for copy in direct(cc, which):
-                copy.start()
-
-    def factors_hand_on(cc):
-        for which in range(2):
-            for p in same_core(cc):
-                factor_copy(which, p, p, p).wait_recv()
-            for copy in handed(cc, which):
-                copy.start()
+    def factors_start(which, cc):
+        for copy in direct(cc, which):
+            copy.start()
+
+    def factors_hand_on(which, cc):
+        for p in same_core(cc):
+            factor_copy(which, p, p, p).wait_recv()
+        for copy in handed(cc, which):
+            copy.start()
 
     def factors_arrive(which, cc):
         for copy in arriving(cc, which):
@@ -113,6 +112,7 @@
             for copy in direct(cc, which) + handed(cc, which):
                 copy.wait_send()
 
+    on_each(functools.partial(factors_start, 0))
     wide = pts[...].astype(F32)
     sq = wide * wide
     sq_hi = sq.astype(BF16)
@@ -126,7 +126,7 @@
     second_copies = spread(cbuf.at[c], "ctr", c, nc, c2s, c2r)
     sent += second_copies
 
-    on_each(factors_start)
+    on_each(functools.partial(factors_start, 1))
 
     def form(owner):
         block = cbuf[owner].astype(F32).reshape(nd, 2, per, half)
@@ -139,6 +139,7 @@
         kt[pl.ds(pl.multiple_of(owner * cb, cb), cb), :] = jnp.exp(exponent).astype(BF16)
 
     form(c)
+    on_each(functools.partial(factors_hand_on, 0))
     for k in range(1, nc):
         second_copies[k - 1].wait_recv()
         form(lax.rem(c - k + nc, nc))
@@ -209,7 +210,7 @@
         return jnp.dot(row, kt[...], preferred_element_type=F32)
 
     label_row = jnp.concatenate([lab[r:r + 1, :] for r in range(n_pts // 128)], axis=1)
-    summed = total(0, to_centres(label_row), lambda: on_each(factors_hand_on))
+    summed = total(0, to_centres(label_row), lambda: on_each(functools.partial(factors_hand_on, 1)))
     on_each(functools.partial(factors_arrive, 0))
     lowered = kernel_solve_transposed(summed / all_points)
     on_each(functools.partial(factors_arrive, 1))

time: 37.7 us -> 33.9 us (0.90)
  Pallas kernels: 36.2 us -> 32.4 us
    pallas_call x1, Pallas kernels: 36.2 us -> 32.4 us  [body(): pl.pallas_call(functools.partial(kernel, nc, nd, flat), out_shape=jax.Sha...]
where the time goes in v3:
time: 33.9 us; the launch traced here: 33.7 us
  Pallas kernels  32.4 us (96%)
  local copies, waits for them, and re-layouts  1.28 us (4%)
    pallas_call x1, Pallas kernels, body(): pl.pallas_call(functools.partial(kernel, nc, nd, flat), out_shape=jax.Sha...  32.4 us
    unnamed x1, local copies, waits for them, and re-layouts  1.28 us

profile of v3, /device:TPU:0, one launch (start us, length us, event | category | flops | bytes accessed | tf_op | source)
XLA Modules:
  0.0 33.7 jit_solution(4076191912727112242)
XLA Ops:
  0.0 32.4 %shard_map.55 = f32[1,1024]{1,0:T(1,128)} custom-call(bf16[1024,256]{1,0:T(8,128)(2,1)} %pts_in.1, bf16[8,128]{1,0:T(8,128)(2,1)} %bitcast.4, s32[1,32]{1,0:T(1,128)} %bitcast.5, f32[128,512]{1,0:T(8,128)} %kf_in.1, f32[128,512]{1,0:T(8,128)} %rf_in.1), custom_call_target="tpu_custom_call" | custom-call | tf_op jit(solution)/shard_map/pallas_call | solution.py:256
  32.4 1.3 %copy.7 = f32[1024]{0:T(1024)} copy(f32[1024]{0:T(1024)} %bitcast.3) | data formatting | bytes 8192

commit v4 on v3

--- a/solution.py
+++ b/solution.py
@@ -215,25 +215,30 @@
     lowered = kernel_solve_transposed(summed / all_points)
     on_each(functools.partial(factors_arrive, 1))
     right_side = ridge_solve_transposed(lowered)
-    beta = jnp.zeros_like(right_side)
+    solved = 0.0
     residual = right_side
     direction = right_side
     norm_now = jnp.sum(residual * residual, axis=1, keepdims=True)
     for iteration in range(ITERS):
         scaled = ridge_solve(direction)
-        lifted = kernel_solve(scaled).astype(BF16)
-        image = to_points(lifted).astype(BF16)
-        summed = total(1 + iteration, to_centres(image))
+        lifted = kernel_solve(scaled)
+        image = to_points(lifted.astype(BF16)).astype(BF16)
+        weighed = to_centres(image)
+        if iteration == ITERS - 1:
+            length = sum(jnp.sum(s * s, axis=0, keepdims=True) for s in scaled)
+            shared = jnp.sum(total(1 + iteration, lifted * weighed), axis=1, keepdims=True)
+            solved = solved + (norm_now / (shared / all_points + RIDGE * length)) * lifted
+            break
+        summed = total(1 + iteration, weighed)
         inner = kernel_solve_transposed(summed / all_points)
         mapped = ridge_solve_transposed([a + RIDGE * s for a, s in zip(inner, scaled)])
         step = norm_now / jnp.sum(direction * mapped, axis=1, keepdims=True)
-        beta = beta + step * direction
+        solved = solved + step * lifted
         residual = residual - step * mapped
         norm_next = jnp.sum(residual * residual, axis=1, keepdims=True)
         direction = residual + (norm_next / norm_now) * direction
         norm_now = norm_next
-    coefficients = kernel_solve(ridge_solve(beta)).astype(BF16)
-    out[...] = to_points(coefficients)
+    out[...] = to_points(solved.astype(BF16))
 
     for copy in sent:
         copy.wait_send()

time: 33.9 us -> 33.6 us (level)
  no operation moved by 1% of the time
where the time goes in v4:
time: 33.6 us; the launch traced here: 33.4 us
  Pallas kernels  32.1 us (96%)
  local copies, waits for them, and re-layouts  1.28 us (4%)
    pallas_call x1, Pallas kernels, body(): pl.pallas_call(functools.partial(kernel, nc, nd, flat), out_shape=jax.Sha...  32.1 us
    unnamed x1, local copies, waits for them, and re-layouts  1.28 us

profile of v4, /device:TPU:0, one launch (start us, length us, event | category | flops | bytes accessed | tf_op | source)
XLA Modules:
  0.0 33.4 jit_solution(15839271591312760670)
XLA Ops:
  0.0 32.1 %shard_map.55 = f32[1,1024]{1,0:T(1,128)} custom-call(bf16[1024,256]{1,0:T(8,128)(2,1)} %pts_in.1, bf16[8,128]{1,0:T(8,128)(2,1)} %bitcast.4, s32[1,32]{1,0:T(1,128)} %bitcast.5, f32[128,512]{1,0:T(8,128)} %kf_in.1, f32[128,512]{1,0:T(8,128)} %rf_in.1), custom_call_target="tpu_custom_call" | custom-call | tf_op jit(solution)/shard_map/pallas_call | solution.py:261
  32.1 1.3 %copy.7 = f32[1024]{0:T(1024)} copy(f32[1024]{0:T(1024)} %bitcast.3) | data formatting | bytes 8192
